TPU v7x, 256 devices: a whole 4x4x8 slice. The times are simulated.
256 devices in a mesh: seq: 16 (over x, z_lo, core), basis: 16 (over z_hi, y).
Axes of the slice: x: 4, y: 4, z: 8 (z_hi: 4, z_lo: 2; z = z_hi * 2 + z_lo), core: 2. Of those that a mesh axis runs over, the one named last changes fastest.
Arguments:
- up_input: bfloat16 [2048, 5120], P('seq'), may hold values from -6 to 6
- up_grad: bfloat16 [2048, 10240], P('seq', 'basis'), may hold values from -6 to 6
- down_input: bfloat16 [2048, 10240], P('seq', 'basis'), may hold values from -6 to 6
- down_grad: bfloat16 [2048, 5120], P('seq'), may hold values from -6 to 6
- width_up: bfloat16 [5120, 5120], P('basis', 'seq'), may hold values from -0.078125 to 0.078125
- width_down: bfloat16 [5120, 5120], P('basis', 'seq'), may hold values from -0.078125 to 0.078125
- hidden_up: bfloat16 [10240, 10240], P('seq', 'basis'), may hold values from -0.0625 to 0.0625
- hidden_down: bfloat16 [10240, 10240], P('seq', 'basis'), may hold values from -0.0625 to 0.0625
- query_up: bfloat16 [6, 10240, 5120], P(None, 'seq', 'basis'), may hold values from -0.0004272461 to 0.0004272461
- query_down: bfloat16 [6, 10240, 5120], P(None, 'seq', 'basis'), may hold values from -0.0004272461 to 0.0004272461
- eigen_up: float32 [10240, 5120], P('seq', 'basis'), may hold values from 0.05 to 20
- eigen_down: float32 [10240, 5120], P('seq', 'basis'), may hold values from 0.05 to 20
Outputs:
- token_scores: float32 [6, 2048], P(None, 'seq')
All inputs are finite; a program needn't handle non-finite values.
Results may differ from a plain program's by a relative error of at most 0.025.
Values may be sent and summed in bfloat16 or wider, within the bound.
A program may use at most 128 MiB of HBM per device.

v0:
```python
import math

import jax
import jax.numpy as jnp
from jax import lax
from jax.sharding import PartitionSpec as P

DAMPING = 0.1


def settle(values):
    return lax.optimization_barrier(values.astype(jnp.bfloat16)).astype(jnp.float32)


def blockwise(inputs, vectors, blocks):
    row_count = inputs.shape[0]
    feature_width = inputs.shape[1] // blocks
    split_inputs = inputs.reshape(row_count, blocks, feature_width)
    split_vectors = vectors.reshape(vectors.shape[0], blocks, feature_width)
    products = jnp.einsum(
        "tkf,jkf->ktj", split_inputs, split_vectors, preferred_element_type=jnp.float32
    )
    return jnp.sum(settle(products), axis=0)


def shards(
    up_input,
    up_grad,
    down_input,
    down_grad,
    width_up,
    width_down,
    hidden_up,
    hidden_down,
    query_up,
    query_down,
    eigen_up,
    eigen_down,
):
    stacked = jnp.stack([up_grad, down_input])
    segment = lax.all_gather(stacked, "seq", axis=1, tiled=True)
    upward = jnp.einsum("tf,if->ti", segment[0], hidden_up, preferred_element_type=jnp.float32)
    downward = jnp.einsum("tf,if->ti", segment[1], hidden_down, preferred_element_type=jnp.float32)
    summands = jnp.concatenate([upward, downward], axis=1)
    hidden_both = lax.psum(summands.astype(jnp.bfloat16), "basis")
    gathered = (
        lax.all_gather(width_up, "seq", axis=1, tiled=True),
        lax.all_gather(width_down, "seq", axis=1, tiled=True),
    )
    blocks = lax.axis_size("seq")
    upward = blockwise(up_input, gathered[0], blocks)
    downward = blockwise(down_grad, gathered[1], blocks)
    local_rows = jnp.concatenate([upward, downward], axis=1).astype(jnp.bfloat16)
    width_both = lax.all_gather(local_rows, "seq", axis=0, tiled=True)
    multiplier_up = (query_up.astype(jnp.float32) / (eigen_up + DAMPING)).astype(jnp.bfloat16)
    multiplier_down = (query_down.astype(jnp.float32) / (eigen_down + DAMPING)).astype(jnp.bfloat16)
    hidden_cols = multiplier_up.shape[1]
    width_cols = multiplier_up.shape[2]
    tokens = hidden_both.shape[0]
    span_rows = math.gcd(tokens, 512)

    def score_block(position):
        offset = position * span_rows
        hidden_block = lax.dynamic_slice_in_dim(hidden_both, offset, span_rows, 0)
        width_block = lax.dynamic_slice_in_dim(width_both, offset, span_rows, 0)
        upward = jnp.einsum(
            "qij,tj->qti",
            multiplier_up,
            width_block[:, :width_cols],
            preferred_element_type=jnp.float32,
        )
        downward = jnp.einsum(
            "qij,tj->qti",
            multiplier_down,
            width_block[:, width_cols:],
            preferred_element_type=jnp.float32,
        )
        first_part = jnp.sum(
            upward * hidden_block[None, :, :hidden_cols].astype(jnp.float32), axis=2
        )
        second_part = jnp.sum(
            downward * hidden_block[None, :, hidden_cols:].astype(jnp.float32), axis=2
        )
        return first_part + second_part

    sections = lax.map(score_block, jnp.arange(tokens // span_rows, dtype=jnp.int32))
    summed_scores = jnp.transpose(sections, (1, 0, 2)).reshape(sections.shape[1], tokens)
    overall = lax.psum(summed_scores, ("seq", "basis"))
    local_count = tokens // lax.axis_size("seq")
    result_scores = lax.dynamic_slice_in_dim(
        overall, lax.axis_index("seq") * local_count, local_count, 1
    )
    return result_scores


def solution(mesh):
    return jax.shard_map(
        shards,
        mesh=mesh,
        in_specs=(
            P("seq", None),
            P("seq", "basis"),
            P("seq", "basis"),
            P("seq", None),
            P("basis", "seq"),
            P("basis", "seq"),
            P("seq", "basis"),
            P("seq", "basis"),
            P(None, "seq", "basis"),
            P(None, "seq", "basis"),
            P("seq", "basis"),
            P("seq", "basis"),
        ),
        out_specs=P(None, "seq"),
        check_vma=False,
    )
```

profile of v0, /device:TPU:32, one launch (start us, length us, event | category | flops | bytes accessed | tf_op | source)
XLA Modules:
  0.0 578.9 jit_solution(7294629523674116413)
XLA Ops:
  6.5 1.9 copy.22
  8.6 1.8 copy.26
  10.5 1.8 pad_maximum_fusion.1
  12.3 1.5 copy.21
  14.5 36.6 %all-gather.5.cloned.1.call-done = bf16[320,5120]{0,1:T(8,128)(2,1)} async-done(((bf16[320,320]{0,1:T(8,128)(2,1)}), bf16[320,5120]{0,1:T(8,128)(2,1)}) %all-gather.5.cloned.1.call-update) | async-done | bytes 3276816 | tf_op jit(solution)/shard_map/all_gather | solution.py:47
  51.1 3.9 convolution_convert_fusion.3
  55.0 37.4 %all-gather.7.cloned.1.call-done = bf16[320,5120]{0,1:T(8,128)(2,1)} async-done(((bf16[320,320]{0,1:T(8,128)(2,1)}), bf16[320,5120]{0,1:T(8,128)(2,1)}) %all-gather.7.cloned.1.call-update) | async-done | bytes 3276816 | tf_op jit(solution)/shard_map/all_gather | solution.py:48
  92.4 4.5 convolution_convert_fusion.2
  97.2 1.5 reduce.3
  99.6 36.4 %all-gather.11.cloned.1.call-done = bf16[2,2048,640]{2,1,0:T(8,128)(2,1)} async-done(((bf16[2,128,640]{2,1,0:T(8,128)(2,1)}), bf16[2,2048,640]{2,1,0:T(8,128)(2,1)}) %all-gather.11.cloned.1.call-update) | async-done | bytes 5242896 | tf_op jit(solution)/shard_map/all_gather | solution.py:41
  136.0 4.1 convolution_convert_fusion
  140.2 2.2 convolution_convert_fusion.1
  142.4 2.8 pad_maximum_fusion
  145.2 1.4 broadcast_add_fusion
  146.6 1.2 broadcast_add_fusion.1
  147.8 5.0 divide_convert_fusion
  152.9 26.5 %all-gather.9.cloned.1.call-done = bf16[2048,640]{0,1:T(8,128)(2,1)} async-done(((bf16[128,640]{0,1:T(8,128)(2,1)}), bf16[2048,640]{0,1:T(8,128)(2,1)}) %all-gather.9.cloned.1.call-update) | async-done | bytes 2621456 | tf_op jit(solution)/shard_map/all_gather | solution.py:54
  179.3 262.0 %all-reduce.2.cloned.1.call-done = bf16[2048,1280]{0,1:T(8,128)(2,1)} async-done(((bf16[2048,1280]{0,1:T(8,128)(2,1)}), bf16[2048,1280]{0,1:T(8,128)(2,1)}) %all-reduce.2.cloned.1.call-update) | async-done | bytes 5242896 | tf_op jit(solution)/shard_map/psum | solution.py:45
  441.3 54.1 %while.10 = (s32[]{:T(128)}, f32[4,6,512]{2,1,0:T(8,128)S(1)}, s32[4]{0:T(128)S(1)}, bf16[2048,640]{0,1:T(8,128)(2,1)}, bf16[6,640,320]{1,2,0:T(8,128)(2,1)}, /*...) while((s32[]{:T(128)}, f32[4,6,512]{2,1,0:T(8,128)S(1)}, ...), condition=%wide.region_6.7_spmd, body=%wide.region_3.6_spmd.sunk | while | flops 2525099008 | bytes 17441000 | solution.py:86
  442.6 1.4 fusion.15
  445.5 4.5 multiply_reduce_fusion.5
  450.4 4.4 multiply_reduce_fusion.4
  456.2 1.4 fusion.15
  459.0 4.5 multiply_reduce_fusion.5
  463.9 4.4 multiply_reduce_fusion.4
  469.7 1.4 fusion.15
  472.6 4.5 multiply_reduce_fusion.5
  477.4 4.4 multiply_reduce_fusion.4
  483.2 1.4 fusion.15
  486.1 4.5 multiply_reduce_fusion.5
  491.0 4.4 multiply_reduce_fusion.4
  495.4 76.4 %psum.15 = f32[6,2048]{1,0:T(8,128)S(1)} all-reduce(f32[6,2048]{1,0:T(8,128)S(1)} %bitcast.52), channel_id=1, replica_groups=mesh['seq'=16,'basis'=16] {'seq','basis'}, use_global_device_ids=true, to_apply=%region_7.8 | all-reduce | flops 12288 | bytes 98304 | tf_op jit(solution)/shard_map/psum | solution.py:88
  (52 shorter events, 12.9 us)
Async XLA Ops:
  6.5 129.5 %copy-start = (bf16[640,640]{1,0:T(8,128)(2,1)S(1)}, bf16[640,640]{1,0:T(8,128)(2,1)}, u32[]{:S(2)}) copy-start(bf16[640,640]{1,0:T(8,128)(2,1)} %param.21) | copy-start | bytes 2457604
  6.5 5.8 copy-start.2
  6.5 7.2 %copy-start.3 = (bf16[128,5120]{1,0:T(8,128)(2,1)S(1)}, bf16[128,5120]{1,0:T(8,128)(2,1)}, u32[]{:S(2)}) copy-start(bf16[128,5120]{1,0:T(8,128)(2,1)} %param.17) | copy-start | bytes 3932164
  6.5 44.6 %all-gather.5.cloned.1.call-start = ((), (), s32[]{:S(2)}) async-start(), calls=%async_computation | async-start | bytes 4177920 | tf_op jit(solution)/shard_map/all_gather | solution.py:47
  8.5 83.9 %all-gather.7.cloned.1.call-start = ((), (), s32[]{:S(2)}) async-start(), calls=%async_computation.1 | async-start | bytes 4177920 | tf_op jit(solution)/shard_map/all_gather | solution.py:48
  10.4 125.6 %all-gather.11.cloned.1.call-start = ((), (), s32[]{:S(2)}) async-start(), calls=%async_computation.3 | async-start | bytes 5570560 | tf_op jit(solution)/shard_map/all_gather | solution.py:41
  12.2 167.1 %all-gather.9.cloned.1.call-start = ((), (), s32[]{:S(2)}) async-start(), calls=%async_computation.2 | async-start | bytes 2785280 | tf_op jit(solution)/shard_map/all_gather | solution.py:54
  99.4 40.7 %copy-start.5 = (bf16[640,640]{1,0:T(8,128)(2,1)S(1)}, bf16[640,640]{1,0:T(8,128)(2,1)}, u32[]{:S(2)}) copy-start(bf16[640,640]{1,0:T(8,128)(2,1)} %param.20) | copy-start | bytes 2457604
  99.4 341.9 %all-reduce.2.cloned.1.call-start = ((), (), s32[]{:S(2)}) async-start(), calls=%async_computation.4 | async-start | bytes 10485760 | tf_op jit(solution)/shard_map/psum | solution.py:45
  136.0 4.1 copy-start.4
  145.2 2.6 copy-start.1
Sparse Core Ops, SparseCore 0:
  9.2 41.8 all-gather.4
  53.0 39.4 all-gather.6
  94.3 41.7 all-gather.10
  137.6 41.6 all-gather.8
  181.8 259.3 all-reduce.1
where the time goes:
time: 581 us; the launch traced here: 579 us
  waiting for transfers between devices  399 us (69%)
  blocking collectives  76.4 us (13%)
  matrix products  50.2 us (9%)
  other arithmetic  19.7 us (3%)
  local copies, waits for them, and re-layouts  17.2 us (3%)
  between operations  13.3 us (2%)
    psum x1, waiting for transfers between devices, shards(): hidden_both = lax.psum(summands.astype(jnp.bfloat16), 'basis')  262 us
    psum x1, blocking collectives, shards(): overall = lax.psum(summed_scores, ('seq', 'basis'))  76.4 us
    all_gather x1, waiting for transfers between devices, shards(): lax.all_gather(width_down, 'seq', axis=1, tiled=True)  37.4 us
    all_gather x1, waiting for transfers between devices, shards(): lax.all_gather(width_up, 'seq', axis=1, tiled=True)  36.6 us
    all_gather x1, waiting for transfers between devices, shards(): segment = lax.all_gather(stacked, 'seq', axis=1, tiled=True)  36.4 us
    all_gather x1, waiting for transfers between devices, shards(): width_both = lax.all_gather(local_rows, 'seq', axis=0, tiled=True)  26.5 us
    dot_general x4, matrix products, score_block(): jnp.einsum('qij,tj->qti', multiplier_down, width_block[:, width_cols:], p...  17.9 us
    dot_general x4, matrix products, score_block(): jnp.einsum('qij,tj->qti', multiplier_up, width_block[:, :width_cols], pre...  17.5 us
  transfers between devices with their start and end apart: 5, of which 5 were waited for; matrix products, arithmetic and copies ran while one was open for 6% of the time, Pallas kernels for 0%

commit v1 on v0

v1 whole, which is shorter than its diff:
```python
import functools

import jax
import jax.numpy as jnp
from jax import lax
from jax.experimental import pallas as pl
from jax.experimental.pallas import tpu as pltpu
from jax.sharding import PartitionSpec as P

DAMPING = 0.1
MESH = pl.DeviceIdType.MESH
F32 = jnp.float32
BF16 = jnp.bfloat16

GROUPS = 8
ITERATIONS = 16


def dot_nt(a, b):
    return lax.dot_general(a, b, (((1,), (1,)), ((), ())), preferred_element_type=F32)


def kernel(
    up_input, up_grad, down_input, down_grad, width_up, width_down, hidden_up, hidden_down,
    query_up, query_down, eigen_up, eigen_down,
    out,
    xg, vh, part, r1, r2, r3, hid, vw, feat, wacc, wg, query, eigen, mult,
    acc, red_c, red_zl, red_x, red_y, red_zh, sum_x, sum_y,
    local_sem, x_send, x_recv, v_send, v_recv, w_send, w_recv,
    h_send, h_recv, red_send, red_recv,
):
    s = lax.axis_index("seq")
    b = lax.axis_index("basis")
    x, zl, c = s // 4, lax.rem(s // 2, 2), lax.rem(s, 2)
    zh, y = b // 4, lax.rem(b, 4)
    x1, x2, x3 = lax.rem(x + 1, 4), lax.rem(x + 2, 4), lax.rem(x + 3, 4)
    y1, y2, y3 = lax.rem(y + 1, 4), lax.rem(y + 2, 4), lax.rem(y + 3, 4)

    def slot(px, pzl, pc):
        return px * 4 + pzl * 2 + pc

    def at_y(py):
        return (s, zh * 4 + py)

    def at_zh(d):
        return (s, lax.rem(zh + d, 4) * 4 + y)

    def at_x(px):
        return (slot(px, zl, c), b)

    to_core = (slot(x, zl, 1 - c), b)
    to_zl = (slot(x, 1 - zl, c), b)

    def remote(src, dst, send, recv, to):
        return pltpu.make_async_remote_copy(
            src_ref=src, dst_ref=dst, send_sem=send, recv_sem=recv, device_id=to, device_id_type=MESH
        )

    moves = [
        (up_grad, xg.at[s, 0]),
        (down_input, xg.at[s, 1]),
        (hidden_up, vh.at[0]),
        (hidden_down, vh.at[1]),
        (width_up, vw.at[s, 0]),
        (width_down, vw.at[s, 1]),
        (query_up, query.at[0]),
        (query_down, query.at[1]),
        (eigen_up, eigen.at[0]),
        (eigen_down, eigen.at[1]),
        (up_input, feat.at[0]),
        (down_grad, feat.at[1]),
    ]
    loads = [pltpu.make_async_copy(a, d, local_sem.at[n]) for n, (a, d) in enumerate(moves)]
    for load in loads:
        load.start()

    barrier = pltpu.get_barrier_semaphore()
    partners = [to_core, to_zl, at_x(x1), at_x(x2), at_x(x3), at_y(y1), at_y(y2), at_y(y3)]
    partners += [at_zh(d) for d in (1, 2, 3)]
    for partner in partners:
        pl.semaphore_signal(barrier, inc=1, device_id=partner, device_id_type=MESH)
    pl.semaphore_wait(barrier, len(partners))

    def place(k):
        px = jnp.where(k < 2, x, jnp.where(k >= 6, x2, jnp.where(lax.rem(k, 2) == 0, x3, x1)))
        high = jnp.where((k == 3) | (k == 4) | (k == 7), 1, 0)
        pzl = jnp.where(k == 0, zl, jnp.where(k == 1, 1 - zl, high))
        return px * 4 + pzl * 2

    def gather_copy(buf, send, recv, k, way, to):
        block = buf.at[place(k) + c]
        return remote(block, block, send.at[way, k], recv.at[place(k) + c], to)

    def gather_send(buf, send, recv, k):
        gather_copy(buf, send, recv, k, 0, to_core).start()

        @pl.when(k == 0)
        def _():
            gather_copy(buf, send, recv, k, 1, to_zl).start()

        @pl.when(k <= 2)
        def _():
            gather_copy(buf, send, recv, k, 2, at_x(x1)).start()

        @pl.when((k <= 1) | (k == 3))
        def _():
            gather_copy(buf, send, recv, k, 3, at_x(x3)).start()

    def gather_wait(buf, send, recv, k):
        gather_copy(buf, send, recv, k, 0, to_core).wait_recv()

    def gather_wait_core(buf, send, recv, k):
        block = buf.at[place(k) + 1 - c]
        remote(block, block, send.at[0, k], recv.at[place(k) + 1 - c], to_core).wait_recv()

    def gather_step(buf, send, recv, k):
        @pl.when(k > 0)
        def _():
            gather_wait(buf, send, recv, k)

        gather_send(buf, send, recv, k)

    def gather_drain(buf, send, recv):
        def body(k, _):
            gather_copy(buf, send, recv, k, 0, to_core).wait_send()

            @pl.when(k == 0)
            def _():
                gather_copy(buf, send, recv, k, 1, to_zl).wait_send()

            @pl.when(k <= 2)
            def _():
                gather_copy(buf, send, recv, k, 2, at_x(x1)).wait_send()

            @pl.when((k <= 1) | (k == 3))
            def _():
                gather_copy(buf, send, recv, k, 3, at_x(x3)).wait_send()

            return 0

        lax.fori_loop(0, GROUPS, body, 0)

    x_gather = (xg, x_send, x_recv)
    v_gather = (vw, v_send, v_recv)
    w_gather = (wg, w_send, w_recv)

    def rows(py, first, count):
        return pl.ds(pl.multiple_of(py * 64 + first, 16), count)

    def h_copy(k, n):
        sems = (h_send.at[k, n], h_recv.at[k, n])
        if n == 0:
            return remote(part.at[k, rows(y2, 0, 32)], r1.at[k, 0], *sems, at_y(y1))
        if n == 1:
            return remote(part.at[k, rows(y2, 32, 32)], r1.at[k, 1], *sems, at_y(y3))
        if n == 2:
            return remote(part.at[k, rows(y1, 32, 32)], r2.at[k, 0, pl.ds(32, 32)], *sems, at_y(y1))
        if n == 3:
            return remote(part.at[k, rows(y3, 0, 32)], r2.at[k, 1, pl.ds(0, 32)], *sems, at_y(y3))
        if n == 4:
            return remote(part.at[k, rows(y1, 0, 32)], r2.at[k, 0, pl.ds(0, 32)], *sems, at_y(y1))
        if n == 5:
            return remote(part.at[k, rows(y3, 32, 32)], r2.at[k, 1, pl.ds(32, 32)], *sems, at_y(y3))
        if n < 9:
            d = n - 5
            piece = part.at[k, rows(y, lax.rem(zh + d, 4) * 16, 16)]
            return remote(piece, r3.at[k, d - 1], *sems, at_zh(d))
        if n < 12:
            d = n - 8
            piece = hid.at[k, rows(y, zh * 16, 16)]
            return remote(piece, piece, *sems, at_zh(d))
        if n == 12:
            piece, to = hid.at[k, rows(y, 0, 32)], at_y(y1)
        elif n == 13:
            piece, to = hid.at[k, rows(y, 32, 32)], at_y(y3)
        elif n == 14:
            piece, to = hid.at[k, rows(y, 32, 32)], at_y(y1)
        elif n == 15:
            piece, to = hid.at[k, rows(y, 0, 32)], at_y(y3)
        elif n == 16:
            piece, to = hid.at[k, rows(y3, 0, 32)], at_y(y1)
        else:
            piece, to = hid.at[k, rows(y1, 32, 32)], at_y(y3)
        return remote(piece, piece, *sems, to)

    def h_wait(k, n):
        if n == 0:
            dst = r1.at[k, 0]
        elif n == 1:
            dst = r1.at[k, 1]
        elif n in (2, 4):
            dst = r2.at[k, 0, pl.ds(32 if n == 2 else 0, 32)]
        elif n in (3, 5):
            dst = r2.at[k, 1, pl.ds(0 if n == 3 else 32, 32)]
        elif n < 9:
            dst = r3.at[k, n - 6]
        elif n < 12:
            dst = hid.at[k, rows(y, lax.rem(zh + 4 - (n - 8), 4) * 16, 16)]
        elif n == 12:
            dst = hid.at[k, rows(y3, 0, 32)]
        elif n == 13:
            dst = hid.at[k, rows(y1, 32, 32)]
        elif n == 14:
            dst = hid.at[k, rows(y3, 32, 32)]
        elif n == 15:
            dst = hid.at[k, rows(y1, 0, 32)]
        elif n == 16:
            dst = hid.at[k, rows(y2, 0, 32)]
        else:
            dst = hid.at[k, rows(y2, 32, 32)]
        remote(dst, dst, h_send.at[k, n], h_recv.at[k, n], at_y(y1)).wait_recv()

    def stage_partial(k):
        gather_wait_core(*x_gather, k)
        first = place(k)
        for p in range(2):
            rows_in = xg[pl.ds(first, 2), p].reshape(256, 640)
            part[k, :, pl.ds(p * 640, 640)] = dot_nt(rows_in, vh[p]).astype(BF16)
        for n in (0, 1, 2, 3):
            h_copy(k, n).start()

    def stage_near(k):
        h_wait(k, 0)
        span = rows(y1, 0, 32)
        part[k, span, :] = (part[k, span, :].astype(F32) + r1[k, 0].astype(F32)).astype(BF16)
        h_copy(k, 4).start()
        h_wait(k, 1)
        span = rows(y3, 32, 32)
        part[k, span, :] = (part[k, span, :].astype(F32) + r1[k, 1].astype(F32)).astype(BF16)
        h_copy(k, 5).start()

    def stage_own(k):
        for n in (2, 3, 4, 5):
            h_wait(k, n)
        span = rows(y, 0, 64)
        total = part[k, span, :].astype(F32) + r2[k, 0].astype(F32) + r2[k, 1].astype(F32)
        part[k, span, :] = total.astype(BF16)
        for n in (7, 6, 8):
            h_copy(k, n).start()

    def stage_sum(k):
        for n in (6, 7, 8):
            h_wait(k, n)
        span = rows(y, zh * 16, 16)
        total = part[k, span, :].astype(F32)
        for d in range(3):
            total = total + r3[k, d].astype(F32)
        hid[k, span, :] = total.astype(BF16)
        for n in (10, 9, 11):
            h_copy(k, n).start()

    def stage_spread(k):
        for n in (9, 10, 11):
            h_wait(k, n)
        for n in (12, 13, 14, 15):
            h_copy(k, n).start()

    def stage_forward(k):
        h_wait(k, 12)
        h_copy(k, 16).start()
        h_wait(k, 13)
        h_copy(k, 17).start()

    def stage_arrive(k):
        for n in (14, 15, 16, 17):
            h_wait(k, n)

    def width_part(k):
        gather_wait_core(*v_gather, k)
        first = place(k)
        span = pl.ds(pl.multiple_of(first // 2 * 640, 640), 640)
        for p in range(2):
            block = feat[p, :, span]
            add = dot_nt(block[:, :320], vw[first, p]) + dot_nt(block[:, 320:], vw[first + 1, p])
            wacc[p] = wacc[p] + add

    def prepare(n):
        p = n // 3
        j = lax.rem(n, 3)

        def body(r, _):
            span = pl.ds(pl.multiple_of(r * 64, 64), 64)
            scale = 1.0 / (eigen[p, span, :] + DAMPING)
            even = (query[p, 2 * j, span, :].astype(F32) * scale).astype(BF16)
            odd = (query[p, 2 * j + 1, span, :].astype(F32) * scale).astype(BF16)
            mult[p, j, span, :] = jnp.concatenate([even, odd], axis=1)
            return 0

        lax.fori_loop(0, 10, body, 0)

    lane = lax.broadcasted_iota(jnp.int32, (256, 128), 1)

    def score(k):
        first = place(k)
        twice = []
        for p in range(2):
            w = wg[pl.ds(first, 2), p].reshape(256, 320).astype(F32)
            twice.append(jnp.concatenate([w, w], axis=1))

        def body(j, table):
            total = jnp.zeros((256, 640), F32)
            for p in range(2):
                product = jnp.dot(
                    hid[k, :, pl.ds(p * 640, 640)], mult[p, j], preferred_element_type=F32
                )
                total = total + product * twice[p]
            tiles = [total[:, n * 128:(n + 1) * 128] for n in range(5)]
            even = tiles[0] + tiles[1] + jnp.where(lane < 64, tiles[2], 0.0)
            odd = tiles[3] + tiles[4] + jnp.where(lane < 64, 0.0, tiles[2])
            even = jnp.sum(even, axis=1, keepdims=True)
            odd = jnp.sum(odd, axis=1, keepdims=True)
            return table + jnp.where(lane == 2 * j, even, 0.0) + jnp.where(lane == 2 * j + 1, odd, 0.0)

        table = lax.fori_loop(0, 3, body, jnp.zeros((256, 128), F32))
        flat = jnp.transpose(table)[:8]
        px, pzl = first // 4, lax.rem(first // 2, 2)
        acc[0, pzl, px] = flat[:, :128]
        acc[1, pzl, px] = flat[:, 128:]

    wacc[...] = jnp.zeros_like(wacc)
    for n in (0, 1):
        loads[n].wait()
    gather_send(*x_gather, 0)
    for n in (4, 5):
        loads[n].wait()
    gather_send(*v_gather, 0)
    for n in (2, 3, 6, 7, 8, 9, 10, 11):
        loads[n].wait()

    def at(i, offset, stage):
        @pl.when((i >= offset) & (i < offset + GROUPS))
        def _():
            stage(i - offset)

    def x_step(k):
        @pl.when(k > 0)
        def _():
            gather_step(*x_gather, k)

    def v_step(k):
        @pl.when(k > 0)
        def _():
            gather_step(*v_gather, k)

    def iteration(i, _):
        at(i, 0, x_step)
        at(i, 0, stage_partial)
        at(i, 1, stage_near)
        at(i, 2, stage_own)

        @pl.when((i >= 1) & (i < 7))
        def _():
            prepare(i - 1)

        at(i, 2, v_step)
        at(i, 3, stage_sum)
        at(i, 3, width_part)
        at(i, 4, stage_spread)
        at(i, 5, stage_forward)
        at(i, 6, stage_arrive)

        @pl.when(i == 10)
        def _():
            wg[s] = wacc[...].astype(BF16)
            gather_send(*w_gather, 0)

        @pl.when(i == 11)
        def _():
            gather_step(*w_gather, 1)

        @pl.when(i == 12)
        def _():
            def body(k, _):
                gather_step(*w_gather, k)
                return 0

            lax.fori_loop(2, GROUPS, body, 0)

            def twin(k, _):
                gather_wait_core(*w_gather, k)
                return 0

            lax.fori_loop(0, GROUPS, twin, 0)

        @pl.when(i >= 12)
        def _():
            def body(k, _):
                score(k)
                return 0

            low = jnp.where(i == 12, 0, i - 6)
            high = jnp.where(i > 13, 0, i - 5)
            lax.fori_loop(low, high, body, 0)

        return 0

    lax.fori_loop(0, 14, iteration, 0)

    copy = remote(acc.at[1 - c], red_c, red_send.at[0], red_recv.at[0], to_core)
    copy.start()
    copy.wait()
    acc[c] = acc[c] + red_c[...]
    copy = remote(acc.at[c, 1 - zl], red_zl, red_send.at[1], red_recv.at[1], to_zl)
    copy.start()
    copy.wait()
    acc[c, zl] = acc[c, zl] + red_zl[...]
    copies = [
        remote(acc.at[c, zl, px], red_x.at[n], red_send.at[2 + n], red_recv.at[2 + n], at_x(px))
        for n, px in enumerate((x1, x2, x3))
    ]
    for copy in copies:
        copy.start()
    for copy in copies:
        copy.wait()
    sum_x[...] = acc[c, zl, x] + red_x[0] + red_x[1] + red_x[2]
    copies = [
        remote(sum_x, red_y.at[n], red_send.at[5 + n], red_recv.at[5 + n], at_y(py))
        for n, py in enumerate((y1, y2, y3))
    ]
    for copy in copies:
        copy.start()
    for copy in copies:
        copy.wait()
    sum_y[...] = sum_x[...] + red_y[0] + red_y[1] + red_y[2]
    copies = [
        remote(sum_y, red_zh.at[n], red_send.at[8 + n], red_recv.at[8 + n], at_zh(n + 1))
        for n in range(3)
    ]
    for copy in copies:
        copy.start()
    for copy in copies:
        copy.wait()
    out[...] = (sum_y[...] + red_zh[0] + red_zh[1] + red_zh[2])[:6]

    for gather in (x_gather, v_gather, w_gather):
        gather_drain(*gather)

    def drain(k, _):
        for n in range(18):
            h_copy(k, n).wait_send()
        return 0

    lax.fori_loop(0, GROUPS, drain, 0)


def shards(*blocks):
    vmem = pltpu.VMEM
    return pl.pallas_call(
        kernel,
        out_shape=jax.ShapeDtypeStruct((6, 128), F32),
        in_specs=[pl.BlockSpec(memory_space=pl.ANY)] * 12,
        out_specs=pl.BlockSpec(memory_space=pltpu.VMEM),
        scratch_shapes=[
            vmem((16, 2, 128, 640), BF16),
            vmem((2, 640, 640), BF16),
            vmem((GROUPS, 256, 1280), BF16),
            vmem((GROUPS, 2, 32, 1280), BF16),
            vmem((GROUPS, 2, 64, 1280), BF16),
            vmem((GROUPS, 3, 16, 1280), BF16),
            vmem((GROUPS, 256, 1280), BF16),
            vmem((16, 2, 320, 320), BF16),
            vmem((2, 128, 5120), BF16),
            vmem((2, 128, 320), F32),
            vmem((16, 2, 128, 320), BF16),
            vmem((2, 6, 640, 320), BF16),
            vmem((2, 640, 320), F32),
            vmem((2, 3, 640, 640), BF16),
            vmem((2, 2, 4, 8, 128), F32),
            vmem((2, 4, 8, 128), F32),
            vmem((4, 8, 128), F32),
            vmem((3, 8, 128), F32),
            vmem((3, 8, 128), F32),
            vmem((3, 8, 128), F32),
            vmem((8, 128), F32),
            vmem((8, 128), F32),
            pltpu.SemaphoreType.DMA((12,)),
            pltpu.SemaphoreType.DMA((4, GROUPS)),
            pltpu.SemaphoreType.DMA((16,)),
            pltpu.SemaphoreType.DMA((4, GROUPS)),
            pltpu.SemaphoreType.DMA((16,)),
            pltpu.SemaphoreType.DMA((4, GROUPS)),
            pltpu.SemaphoreType.DMA((16,)),
            pltpu.SemaphoreType.DMA((GROUPS, 18)),
            pltpu.SemaphoreType.DMA((GROUPS, 18)),
            pltpu.SemaphoreType.DMA((11,)),
            pltpu.SemaphoreType.DMA((11,)),
        ],
        compiler_params=pltpu.CompilerParams(
            collective_id=0, has_side_effects=True, vmem_limit_bytes=60 * 1024 * 1024
        ),
        cost_estimate=pl.CostEstimate(flops=14_000_000_000, bytes_accessed=12_000_000, transcendentals=0),
    )(*blocks)


def solution(mesh):
    return jax.shard_map(
        shards,
        mesh=mesh,
        in_specs=(
            P("seq", None),
            P("seq", "basis"),
            P("seq", "basis"),
            P("seq", None),
            P("basis", "seq"),
            P("basis", "seq"),
            P("seq", "basis"),
            P("seq", "basis"),
            P(None, "seq", "basis"),
            P(None, "seq", "basis"),
            P("seq", "basis"),
            P("seq", "basis"),
        ),
        out_specs=P(None, "seq"),
        check_vma=False,
    )
```

time: 581 us -> 186 us (0.32)
  waiting for transfers between devices: 399 us -> 0 us
  Pallas kernels: 0 us -> 171 us
  blocking collectives: 76.4 us -> 0 us
  matrix products: 50.2 us -> 0 us
  other arithmetic: 19.7 us -> 0 us
  between operations: 13.3 us -> 0.01 us
    psum x1 -> x0, waiting for transfers between devices: 262 us -> none  [shards(): hidden_both = lax.psum(summands.astype(jnp.bfloat16), 'basis')]
    pallas_call x0 -> x1, Pallas kernels: none -> 171 us  [shards(): pl.pallas_call(kernel, out_shape=jax.ShapeDtypeStruct((6, 128), F32), in_...]
    all_gather x4 -> x0, waiting for transfers between devices: 137 us -> none  [the longest x1 37.4 us: shards(): lax.all_gather(width_down, 'seq', axis=1, tiled=True)]
    psum x1 -> x0, blocking collectives: 76.4 us -> none  [shards(): overall = lax.psum(summed_scores, ('seq', 'basis'))]
    dot_general x12 -> x0, matrix products: 50.2 us -> none  [the longest x4 17.9 us: score_block(): jnp.einsum('qij,tj->qti', multiplier_down, width_block[:, width_cols:], p...]
    convert_element_type x9 -> x0, other arithmetic: 10.2 us -> none  [the longest x1 5.03 us: shards(): (query_down.astype(jnp.float32) / (eigen_down + DAMPING)).astype(jnp.bflo...]
    unnamed x16 -> x7, local copies, waits for them, and re-layouts: 6.01 us -> 15.1 us
  transfers between devices with their start and end apart: 5 -> 0, of which waited for: 5 -> 0; matrix products, arithmetic and copies ran while one was open for 6% -> 0% of each run, Pallas kernels for 0% -> 0%
where the time goes in v1:
time: 186 us
  Pallas kernels  171 us (92%)
  local copies, waits for them, and re-layouts  15.1 us (8%)
    pallas_call x1, Pallas kernels, shards(): pl.pallas_call(kernel, out_shape=jax.ShapeDtypeStruct((6, 128), F32), in_...  171 us
    unnamed x7, local copies, waits for them, and re-layouts  15.1 us

profile of v1, /device:TPU:32, one launch (start us, length us, event | category | flops | bytes accessed | tf_op | source)
XLA Modules:
  0.0 185.6 jit_solution(14567721022940080987)
XLA Ops:
  0.0 0.0 copy-start
  0.0 2.6 %copy.15.eigen_up = f32[640,320]{1,0:T(8,128)} copy(f32[640,320]{0,1:T(8,128)} %param.22) | data formatting | bytes 1638400 | tf_op args[10]
  2.6 2.4 %copy.16.eigen_down = f32[640,320]{1,0:T(8,128)} copy(f32[640,320]{0,1:T(8,128)} %param.23) | data formatting | bytes 1638400 | tf_op args[11]
  5.0 0.0 copy-done
  5.0 3.5 %copy.13.query_up = bf16[6,640,320]{2,1,0:T(8,128)(2,1)} copy(bf16[6,640,320]{1,2,0:T(8,128)(2,1)S(1)} %copy-done) | data formatting | bytes 4915200 | tf_op args[8]
  8.5 5.3 %copy.14.query_down = bf16[6,640,320]{2,1,0:T(8,128)(2,1)} copy(bf16[6,640,320]{1,2,0:T(8,128)(2,1)} %param.21) | data formatting | bytes 4915200 | tf_op args[9]
  13.8 170.5 %shard_map.118 = f32[6,128]{1,0:T(8,128)} custom-call(bf16[128,5120]{1,0:T(8,128)(2,1)} %up_input.1, bf16[128,640]{1,0:T(8,128)(2,1)} %up_grad.1, bf16[128,640]{1,0:T(8,128)(2,1)} %down_input.1, bf16[128,5120]{1,0:T(8,128)(2,1)} %down_grad.1, bf16[320,320]{1,0:T(8,128)(2,1)} %width_up.1, bf16[320,320]{1,0:T(8,128)(2,1)} %width_down.1, ...), custom_call_target="tpu_custom_call" | custom-call | flops 14000000000 | bytes 12000000 | tf_op jit(solution)/shard_map/pallas_call | solution.py:448
  184.3 1.3 copy.18
Async XLA Ops:
  0.0 5.0 %copy-start = (bf16[6,640,320]{1,2,0:T(8,128)(2,1)S(1)}, bf16[6,640,320]{1,2,0:T(8,128)(2,1)}, u32[]{:S(2)}) copy-start(bf16[6,640,320]{1,2,0:T(8,128)(2,1)} %param.20) | copy-start | bytes 7372804

commit v2 on v1

--- a/solution.py
+++ b/solution.py
@@ -13,7 +13,14 @@
 BF16 = jnp.bfloat16
 
 GROUPS = 8
-ITERATIONS = 16
+ORDER = "gfedcbaws"
+O_X, O_PART, O_NEAR, O_OWN, O_SUM, O_SPREAD, O_FORWARD, O_ARRIVE, O_SCORE = 0, 0, 1, 2, 3, 4, 5, 6, 9
+RATE = 2
+V_MARKS = ((2, 2), (3, 4), (5, 6), (6, 8))
+VC_MARKS = ((3, 2), (4, 4), (6, 6), (7, 8))
+W_START = 7
+W_MARKS = ((8, 2), (9, 8))
+WC_MARKS = ((9, 8),)
 
 
 def dot_nt(a, b):
@@ -83,9 +90,8 @@
 
     def place(k):
         px = jnp.where(k < 2, x, jnp.where(k >= 6, x2, jnp.where(lax.rem(k, 2) == 0, x3, x1)))
-        high = jnp.where((k == 3) | (k == 4) | (k == 7), 1, 0)
-        pzl = jnp.where(k == 0, zl, jnp.where(k == 1, 1 - zl, high))
-        return px * 4 + pzl * 2
+        own = (k == 0) | (k == 2) | (k == 3) | (k == 6)
+        return px * 4 + jnp.where(own, zl, 1 - zl) * 2
 
     def gather_copy(buf, send, recv, k, way, to):
         block = buf.at[place(k) + c]
@@ -102,7 +108,7 @@
         def _():
             gather_copy(buf, send, recv, k, 2, at_x(x1)).start()
 
-        @pl.when((k <= 1) | (k == 3))
+        @pl.when((k <= 1) | (k == 5))
         def _():
             gather_copy(buf, send, recv, k, 3, at_x(x3)).start()
 
@@ -132,7 +138,7 @@
             def _():
                 gather_copy(buf, send, recv, k, 2, at_x(x1)).wait_send()
 
-            @pl.when((k <= 1) | (k == 3))
+            @pl.when((k <= 1) | (k == 5))
             def _():
                 gather_copy(buf, send, recv, k, 3, at_x(x3)).wait_send()
 
@@ -274,16 +280,12 @@
             add = dot_nt(block[:, :320], vw[first, p]) + dot_nt(block[:, 320:], vw[first + 1, p])
             wacc[p] = wacc[p] + add
 
-    def prepare(n):
-        p = n // 3
-        j = lax.rem(n, 3)
-
+    def prepare(p):
         def body(r, _):
-            span = pl.ds(pl.multiple_of(r * 64, 64), 64)
+            span = pl.ds(pl.multiple_of(r * 32, 32), 32)
             scale = 1.0 / (eigen[p, span, :] + DAMPING)
-            even = (query[p, 2 * j, span, :].astype(F32) * scale).astype(BF16)
-            odd = (query[p, 2 * j + 1, span, :].astype(F32) * scale).astype(BF16)
-            mult[p, j, span, :] = jnp.concatenate([even, odd], axis=1)
+            for q in range(6):
+                mult[p, q, span, :] = (query[p, q, span, :].astype(F32) * scale).astype(BF16)
             return 0
 
         lax.fori_loop(0, 10, body, 0)
@@ -300,8 +302,8 @@
         def body(j, table):
             total = jnp.zeros((256, 640), F32)
             for p in range(2):
-                product = jnp.dot(
-                    hid[k, :, pl.ds(p * 640, 640)], mult[p, j], preferred_element_type=F32
+                product = dot_nt(
+                    hid[k, :, pl.ds(p * 640, 640)], mult[p, pl.ds(2 * j, 2)].reshape(640, 640)
                 )
                 total = total + product * twice[p]
             tiles = [total[:, n * 128:(n + 1) * 128] for n in range(5)]
@@ -324,7 +326,7 @@
     for n in (4, 5):
         loads[n].wait()
     gather_send(*v_gather, 0)
-    for n in (2, 3, 6, 7, 8, 9, 10, 11):
+    for n in (2, 3):
         loads[n].wait()
 
     def at(i, offset, stage):
@@ -332,69 +334,90 @@
         def _():
             stage(i - offset)
 
+    def loop(low, high, stage):
+        def body(k, _):
+            stage(k)
+            return 0
+
+        lax.fori_loop(low, high, body, 0)
+
     def x_step(k):
         @pl.when(k > 0)
         def _():
             gather_step(*x_gather, k)
 
     def v_step(k):
-        @pl.when(k > 0)
-        def _():
-            gather_step(*v_gather, k)
-
-    def iteration(i, _):
-        at(i, 0, x_step)
-        at(i, 0, stage_partial)
-        at(i, 1, stage_near)
-        at(i, 2, stage_own)
-
-        @pl.when((i >= 1) & (i < 7))
-        def _():
-            prepare(i - 1)
-
-        at(i, 2, v_step)
-        at(i, 3, stage_sum)
-        at(i, 3, width_part)
-        at(i, 4, stage_spread)
-        at(i, 5, stage_forward)
-        at(i, 6, stage_arrive)
-
-        @pl.when(i == 10)
+        gather_step(*v_gather, k)
+
+    def w_step(k):
+        gather_step(*w_gather, k)
+
+    def w_twin(k):
+        gather_wait_core(*w_gather, k)
+
+    def bounds(i, marks):
+        low, high = 0, 0
+        for mark, value in marks:
+            low = jnp.where(i > mark, value, low)
+            high = jnp.where(i >= mark, value, high)
+        return low, high
+
+    def run_width(i):
+        low, high = bounds(i, V_MARKS)
+        loop(jnp.maximum(low, 1), high, v_step)
+        low, high = bounds(i, VC_MARKS)
+        loop(low, high, width_part)
+
+        @pl.when(i == W_START)
         def _():
             wg[s] = wacc[...].astype(BF16)
             gather_send(*w_gather, 0)
 
-        @pl.when(i == 11)
-        def _():
-            gather_step(*w_gather, 1)
-
-        @pl.when(i == 12)
-        def _():
-            def body(k, _):
-                gather_step(*w_gather, k)
-                return 0
-
-            lax.fori_loop(2, GROUPS, body, 0)
-
-            def twin(k, _):
-                gather_wait_core(*w_gather, k)
-                return 0
-
-            lax.fori_loop(0, GROUPS, twin, 0)
-
-        @pl.when(i >= 12)
-        def _():
-            def body(k, _):
-                score(k)
-                return 0
-
-            low = jnp.where(i == 12, 0, i - 6)
-            high = jnp.where(i > 13, 0, i - 5)
-            lax.fori_loop(low, high, body, 0)
+        low, high = bounds(i, W_MARKS)
+        loop(jnp.maximum(low, 1), high, w_step)
+        low, high = bounds(i, WC_MARKS)
+        loop(low, high, w_twin)
+
+    def run_score(i):
+        def done(n):
+            return jnp.clip(jnp.minimum(n - O_ARRIVE + 1, RATE * (n - O_SCORE + 1)), 0, GROUPS)
+
+        loop(done(i - 1), done(i), score)
+
+    def iteration(i, _):
+        for stage in ORDER:
+            if stage == "a":
+                at(i, O_X, x_step)
+                at(i, O_PART, stage_partial)
+            if stage == "b":
+                at(i, O_NEAR, stage_near)
+            if stage == "c":
+                at(i, O_OWN, stage_own)
+            if stage == "d":
+                at(i, O_SUM, stage_sum)
+            if stage == "e":
+                at(i, O_SPREAD, stage_spread)
+            if stage == "f":
+                at(i, O_FORWARD, stage_forward)
+            if stage == "g":
+                at(i, O_ARRIVE, stage_arrive)
+            if stage == "w":
+                run_width(i)
+            if stage == "s":
+                run_score(i)
+
+        @pl.when(i == 0)
+        def _():
+            for n in (6, 7, 8, 9, 10, 11):
+                loads[n].wait()
+
+        @pl.when((i == 2) | (i == 3))
+        def _():
+            prepare(i - 2)
 
         return 0
 
-    lax.fori_loop(0, 14, iteration, 0)
+    lax.fori_loop(0, O_ARRIVE + GROUPS, iteration, 0)
 
     copy = remote(acc.at[1 - c], red_c, red_send.at[0], red_recv.at[0], to_core)
     copy.start()
@@ -445,6 +468,7 @@
 
 def shards(*blocks):
     vmem = pltpu.VMEM
+    blocks = blocks[:8] + tuple(jnp.swapaxes(block, -1, -2) for block in blocks[8:])
     return pl.pallas_call(
         kernel,
         out_shape=jax.ShapeDtypeStruct((6, 128), F32),
@@ -462,9 +486,9 @@
             vmem((2, 128, 5120), BF16),
             vmem((2, 128, 320), F32),
             vmem((16, 2, 128, 320), BF16),
-            vmem((2, 6, 640, 320), BF16),
-            vmem((2, 640, 320), F32),
-            vmem((2, 3, 640, 640), BF16),
+            vmem((2, 6, 320, 640), BF16),
+            vmem((2, 320, 640), F32),
+            vmem((2, 6, 320, 640), BF16),
             vmem((2, 2, 4, 8, 128), F32),
             vmem((2, 4, 8, 128), F32),
             vmem((4, 8, 128), F32),

time: 186 us -> 143 us (0.77)
  Pallas kernels: 171 us -> 142 us
  local copies, waits for them, and re-layouts: 15.1 us -> 1.28 us
    pallas_call x1, Pallas kernels: 171 us -> 142 us  [shards(): pl.pallas_call(kernel, out_shape=jax.ShapeDtypeStruct((6, 128), F32), in_...]
    unnamed x7 -> x1, local copies, waits for them, and re-layouts: 15.1 us -> 1.28 us
where the time goes in v2:
time: 143 us
  Pallas kernels  142 us (99%)
    pallas_call x1, Pallas kernels, shards(): pl.pallas_call(kernel, out_shape=jax.ShapeDtypeStruct((6, 128), F32), in_...  142 us

profile of v2, /device:TPU:32, one launch (start us, length us, event | category | flops | bytes accessed | tf_op | source)
XLA Modules:
  0.0 142.8 jit_solution(3920872227753846990)
XLA Ops:
  0.0 141.5 %shard_map.118 = f32[6,128]{1,0:T(8,128)} custom-call(bf16[128,5120]{1,0:T(8,128)(2,1)} %up_input.1, bf16[128,640]{1,0:T(8,128)(2,1)} %up_grad.1, bf16[128,640]{1,0:T(8,128)(2,1)} %down_input.1, bf16[128,5120]{1,0:T(8,128)(2,1)} %down_grad.1, bf16[320,320]{1,0:T(8,128)(2,1)} %width_up.1, bf16[320,320]{1,0:T(8,128)(2,1)} %width_down.1, ...), custom_call_target="tpu_custom_call" | custom-call | flops 14000000000 | bytes 12000000 | tf_op jit(solution)/shard_map/pallas_call | solution.py:472
  141.5 1.3 copy.14

commit v3 on v2

--- a/solution.py
+++ b/solution.py
@@ -12,15 +12,24 @@
 F32 = jnp.float32
 BF16 = jnp.bfloat16
 
+N_SEQ, N_BASIS = 16, 16
 GROUPS = 8
-ORDER = "gfedcbaws"
-O_X, O_PART, O_NEAR, O_OWN, O_SUM, O_SPREAD, O_FORWARD, O_ARRIVE, O_SCORE = 0, 0, 1, 2, 3, 4, 5, 6, 9
+ORDER = "gfedcbawsws"
+O_X, O_PART, O_NEAR, O_OWN, O_SUM, O_SPREAD, O_FORWARD, O_ARRIVE = 0, 0, 1, 2, 3, 4, 5, 6
+VB_START = 3
+VA_MARKS = ((0, 1), (5, 2), (7, 4), (11, 6), (13, 8))
+VB_MARKS = ((0, 1), (9, 2), (11, 4), (15, 6), (17, 8))
+VAC_MARKS = ((0, 0), (7, 2), (9, 4), (13, 6), (15, 8))
+VBC_MARKS = ((0, 0), (13, 2), (15, 4), (17, 6), (19, 8))
+WU_START = 15
+WU_MARKS = ((0, 1), (17, 2), (18, 6), (19, 8))
+WUC_MARKS = ((0, 0), (19, 8))
+WD_START = 19
+WD_MARKS = ((0, 1), (20, 2), (21, 6), (22, 8))
+WDC_MARKS = ((0, 0), (22, 8))
+SU_START = 19
+SD_START = 22
 RATE = 2
-V_MARKS = ((2, 2), (3, 4), (5, 6), (6, 8))
-VC_MARKS = ((3, 2), (4, 4), (6, 6), (7, 8))
-W_START = 7
-W_MARKS = ((8, 2), (9, 8))
-WC_MARKS = ((9, 8),)
 
 
 def dot_nt(a, b):
@@ -31,10 +40,10 @@
     up_input, up_grad, down_input, down_grad, width_up, width_down, hidden_up, hidden_down,
     query_up, query_down, eigen_up, eigen_down,
     out,
-    xg, vh, part, r1, r2, r3, hid, vw, feat, wacc, wg, query, eigen, mult,
-    acc, red_c, red_zl, red_x, red_y, red_zh, sum_x, sum_y,
-    local_sem, x_send, x_recv, v_send, v_recv, w_send, w_recv,
-    h_send, h_recv, red_send, red_recv,
+    xg, vh, part, r1, r2, r3, hid, wide, va, vb, feat, wacc, wu, wd, query, eigen, mult,
+    half, acc, seq_in, seq_sum, basis_in,
+    local_sem, x_send, x_recv, g_send, g_recv,
+    h_send, h_recv, seq_send, seq_recv, basis_send, basis_recv,
 ):
     s = lax.axis_index("seq")
     b = lax.axis_index("basis")
@@ -68,8 +77,8 @@
         (down_input, xg.at[s, 1]),
         (hidden_up, vh.at[0]),
         (hidden_down, vh.at[1]),
-        (width_up, vw.at[s, 0]),
-        (width_down, vw.at[s, 1]),
+        (width_up, wide.at[0]),
+        (width_down, wide.at[1]),
         (query_up, query.at[0]),
         (query_down, query.at[1]),
         (eigen_up, eigen.at[0]),
@@ -82,11 +91,39 @@
         load.start()
 
     barrier = pltpu.get_barrier_semaphore()
-    partners = [to_core, to_zl, at_x(x1), at_x(x2), at_x(x3), at_y(y1), at_y(y2), at_y(y3)]
-    partners += [at_zh(d) for d in (1, 2, 3)]
-    for partner in partners:
-        pl.semaphore_signal(barrier, inc=1, device_id=partner, device_id_type=MESH)
-    pl.semaphore_wait(barrier, len(partners))
+    def prepare(p):
+        def body(r, _):
+            span = pl.ds(pl.multiple_of(r * 32, 32), 32)
+            scale = 1.0 / (eigen[p, span, :] + DAMPING)
+            for q in range(6):
+                mult[p, q, span, :] = (query[p, q, span, :].astype(F32) * scale).astype(BF16)
+            return 0
+
+        lax.fori_loop(0, 10, body, 0)
+
+    others = N_SEQ + N_BASIS - 2
+
+    def along_seq(d):
+        return (lax.rem(s + d, N_SEQ), b)
+
+    def along_basis(d):
+        return (s, lax.rem(b + d, N_BASIS))
+
+    def greet(d, _):
+        pl.semaphore_signal(barrier, inc=1, device_id=along_seq(d), device_id_type=MESH)
+        pl.semaphore_signal(barrier, inc=1, device_id=along_basis(d), device_id_type=MESH)
+        return 0
+
+    lax.fori_loop(1, N_SEQ, greet, 0)
+    for n in (6, 7, 8, 9):
+        loads[n].wait()
+    prepare(0)
+    prepare(1)
+    for n in (4, 5):
+        loads[n].wait()
+    va[s] = jnp.concatenate([wide[0], wide[1, :, 256:]], axis=1)
+    vb[s] = wide[1, :, :256]
+    pl.semaphore_wait(barrier, others)
 
     def place(k):
         px = jnp.where(k < 2, x, jnp.where(k >= 6, x2, jnp.where(lax.rem(k, 2) == 0, x3, x1)))
@@ -147,8 +184,10 @@
         lax.fori_loop(0, GROUPS, body, 0)
 
     x_gather = (xg, x_send, x_recv)
-    v_gather = (vw, v_send, v_recv)
-    w_gather = (wg, w_send, w_recv)
+    va_gather = (va, g_send.at[0], g_recv.at[0])
+    vb_gather = (vb, g_send.at[1], g_recv.at[1])
+    wu_gather = (wu, g_send.at[2], g_recv.at[2])
+    wd_gather = (wd, g_send.at[3], g_recv.at[3])
 
     def rows(py, first, count):
         return pl.ds(pl.multiple_of(py * 64 + first, 16), count)
@@ -271,61 +310,58 @@
         for n in (14, 15, 16, 17):
             h_wait(k, n)
 
-    def width_part(k):
-        gather_wait_core(*v_gather, k)
+    def width_up_part(k):
+        gather_wait_core(*va_gather, k)
         first = place(k)
-        span = pl.ds(pl.multiple_of(first // 2 * 640, 640), 640)
-        for p in range(2):
-            block = feat[p, :, span]
-            add = dot_nt(block[:, :320], vw[first, p]) + dot_nt(block[:, 320:], vw[first + 1, p])
-            wacc[p] = wacc[p] + add
-
-    def prepare(p):
-        def body(r, _):
-            span = pl.ds(pl.multiple_of(r * 32, 32), 32)
-            scale = 1.0 / (eigen[p, span, :] + DAMPING)
-            for q in range(6):
-                mult[p, q, span, :] = (query[p, q, span, :].astype(F32) * scale).astype(BF16)
-            return 0
-
-        lax.fori_loop(0, 10, body, 0)
-
-    lane = lax.broadcasted_iota(jnp.int32, (256, 128), 1)
-
-    def score(k):
+        block = feat[0, :, pl.ds(pl.multiple_of(first // 2 * 640, 640), 640)]
+        for pc in range(2):
+            vectors = va[first + pc][:, :320]
+            wacc[0] = wacc[0] + dot_nt(vectors, block[:, pc * 320:(pc + 1) * 320])
+
+    def width_down_part(k):
+        gather_wait_core(*vb_gather, k)
         first = place(k)
-        twice = []
-        for p in range(2):
-            w = wg[pl.ds(first, 2), p].reshape(256, 320).astype(F32)
-            twice.append(jnp.concatenate([w, w], axis=1))
-
-        def body(j, table):
-            total = jnp.zeros((256, 640), F32)
-            for p in range(2):
-                product = dot_nt(
-                    hid[k, :, pl.ds(p * 640, 640)], mult[p, pl.ds(2 * j, 2)].reshape(640, 640)
-                )
-                total = total + product * twice[p]
-            tiles = [total[:, n * 128:(n + 1) * 128] for n in range(5)]
-            even = tiles[0] + tiles[1] + jnp.where(lane < 64, tiles[2], 0.0)
-            odd = tiles[3] + tiles[4] + jnp.where(lane < 64, 0.0, tiles[2])
-            even = jnp.sum(even, axis=1, keepdims=True)
-            odd = jnp.sum(odd, axis=1, keepdims=True)
-            return table + jnp.where(lane == 2 * j, even, 0.0) + jnp.where(lane == 2 * j + 1, odd, 0.0)
-
-        table = lax.fori_loop(0, 3, body, jnp.zeros((256, 128), F32))
-        flat = jnp.transpose(table)[:8]
-        px, pzl = first // 4, lax.rem(first // 2, 2)
-        acc[0, pzl, px] = flat[:, :128]
-        acc[1, pzl, px] = flat[:, 128:]
+        block = feat[1, :, pl.ds(pl.multiple_of(first // 2 * 640, 640), 640)]
+        for pc in range(2):
+            vectors = jnp.concatenate([vb[first + pc], va[first + pc][:, 320:]], axis=1)
+            wacc[1] = wacc[1] + dot_nt(vectors, block[:, pc * 320:(pc + 1) * 320])
+
+    def scores_copy(k, pc):
+        to = place(k) + pc
+        return remote(acc.at[to], seq_in.at[s], seq_send.at[to], seq_recv.at[s], (to, b))
+
+    def send_scores(k, pc):
+        scores_copy(k, pc).start()
+
+    def score(k, p, table):
+        first = place(k)
+        w = jnp.concatenate([table[first], table[first + 1]], axis=1).astype(F32)
+        h = hid[k, :, pl.ds(p * 640, 640)]
+        lines = []
+        for q in range(6):
+            spread = dot_nt(mult[p, q], h) * w
+            lines.append(jnp.sum(jnp.sum(spread.reshape(40, 8, 256), axis=0), axis=0, keepdims=True))
+        return jnp.concatenate(lines + [jnp.zeros((2, 256), F32)], axis=0)
+
+    def score_up(k):
+        half[k] = score(k, 0, wu)
+
+    def score_down(k):
+        first = place(k)
+        flat = half[k] + score(k, 1, wd)
+        acc[first] = flat[:, :128]
+        acc[first + 1] = flat[:, 128:]
+        send_scores(k, 1 - c)
+
+        @pl.when(k > 0)
+        def _():
+            send_scores(k, c)
 
     wacc[...] = jnp.zeros_like(wacc)
     for n in (0, 1):
         loads[n].wait()
     gather_send(*x_gather, 0)
-    for n in (4, 5):
-        loads[n].wait()
-    gather_send(*v_gather, 0)
+    gather_send(*va_gather, 0)
     for n in (2, 3):
         loads[n].wait()
 
@@ -346,45 +382,57 @@
         def _():
             gather_step(*x_gather, k)
 
-    def v_step(k):
-        gather_step(*v_gather, k)
-
-    def w_step(k):
-        gather_step(*w_gather, k)
-
-    def w_twin(k):
-        gather_wait_core(*w_gather, k)
+    def stepper(gather):
+        return lambda k: gather_step(*gather, k)
+
+    def twins(gather):
+        return lambda k: gather_wait_core(*gather, k)
 
     def bounds(i, marks):
-        low, high = 0, 0
-        for mark, value in marks:
+        low, high = marks[0][1], marks[0][1]
+        for mark, value in marks[1:]:
             low = jnp.where(i > mark, value, low)
             high = jnp.where(i >= mark, value, high)
         return low, high
 
+    def span_loop(i, marks, stage):
+        low, high = bounds(i, marks)
+        loop(low, high, stage)
+
     def run_width(i):
-        low, high = bounds(i, V_MARKS)
-        loop(jnp.maximum(low, 1), high, v_step)
-        low, high = bounds(i, VC_MARKS)
-        loop(low, high, width_part)
-
-        @pl.when(i == W_START)
-        def _():
-            wg[s] = wacc[...].astype(BF16)
-            gather_send(*w_gather, 0)
-
-        low, high = bounds(i, W_MARKS)
-        loop(jnp.maximum(low, 1), high, w_step)
-        low, high = bounds(i, WC_MARKS)
-        loop(low, high, w_twin)
+        @pl.when(i == VB_START)
+        def _():
+            gather_send(*vb_gather, 0)
+
+        span_loop(i, VA_MARKS, stepper(va_gather))
+        span_loop(i, VB_MARKS, stepper(vb_gather))
+        span_loop(i, VAC_MARKS, width_up_part)
+        span_loop(i, VBC_MARKS, width_down_part)
+
+        @pl.when(i == WU_START)
+        def _():
+            wu[s] = wacc[0].astype(BF16)
+            gather_send(*wu_gather, 0)
+
+        @pl.when(i == WD_START)
+        def _():
+            wd[s] = wacc[1].astype(BF16)
+            gather_send(*wd_gather, 0)
+
+        span_loop(i, WU_MARKS, stepper(wu_gather))
+        span_loop(i, WUC_MARKS, twins(wu_gather))
+        span_loop(i, WD_MARKS, stepper(wd_gather))
+        span_loop(i, WDC_MARKS, twins(wd_gather))
 
     def run_score(i):
-        def done(n):
-            return jnp.clip(jnp.minimum(n - O_ARRIVE + 1, RATE * (n - O_SCORE + 1)), 0, GROUPS)
-
-        loop(done(i - 1), done(i), score)
+        def done(n, start):
+            return jnp.clip(jnp.minimum(n // 2 - O_ARRIVE + 1, RATE * (n - start + 1)), 0, GROUPS)
+
+        loop(done(i - 1, SU_START), done(i, SU_START), score_up)
+        loop(done(i - 1, SD_START), done(i, SD_START), score_down)
 
     def iteration(i, _):
+        halves = 0
         for stage in ORDER:
             if stage == "a":
                 at(i, O_X, x_step)
@@ -402,68 +450,50 @@
             if stage == "g":
                 at(i, O_ARRIVE, stage_arrive)
             if stage == "w":
-                run_width(i)
+                run_width(2 * i + halves)
             if stage == "s":
-                run_score(i)
+                run_score(2 * i + halves)
+                halves += 1
 
         @pl.when(i == 0)
         def _():
-            for n in (6, 7, 8, 9, 10, 11):
+            for n in (10, 11):
                 loads[n].wait()
 
-        @pl.when((i == 2) | (i == 3))
-        def _():
-            prepare(i - 2)
-
         return 0
 
     lax.fori_loop(0, O_ARRIVE + GROUPS, iteration, 0)
 
-    copy = remote(acc.at[1 - c], red_c, red_send.at[0], red_recv.at[0], to_core)
-    copy.start()
-    copy.wait()
-    acc[c] = acc[c] + red_c[...]
-    copy = remote(acc.at[c, 1 - zl], red_zl, red_send.at[1], red_recv.at[1], to_zl)
-    copy.start()
-    copy.wait()
-    acc[c, zl] = acc[c, zl] + red_zl[...]
-    copies = [
-        remote(acc.at[c, zl, px], red_x.at[n], red_send.at[2 + n], red_recv.at[2 + n], at_x(px))
-        for n, px in enumerate((x1, x2, x3))
-    ]
-    for copy in copies:
-        copy.start()
-    for copy in copies:
-        copy.wait()
-    sum_x[...] = acc[c, zl, x] + red_x[0] + red_x[1] + red_x[2]
-    copies = [
-        remote(sum_x, red_y.at[n], red_send.at[5 + n], red_recv.at[5 + n], at_y(py))
-        for n, py in enumerate((y1, y2, y3))
-    ]
-    for copy in copies:
-        copy.start()
-    for copy in copies:
-        copy.wait()
-    sum_y[...] = sum_x[...] + red_y[0] + red_y[1] + red_y[2]
-    copies = [
-        remote(sum_y, red_zh.at[n], red_send.at[8 + n], red_recv.at[8 + n], at_zh(n + 1))
-        for n in range(3)
-    ]
-    for copy in copies:
-        copy.start()
-    for copy in copies:
-        copy.wait()
-    out[...] = (sum_y[...] + red_zh[0] + red_zh[1] + red_zh[2])[:6]
-
-    for gather in (x_gather, v_gather, w_gather):
+    seq_in[s] = acc[s]
+    for d in range(1, N_SEQ):
+        other = lax.rem(s + d, N_SEQ)
+        remote(acc.at[other], seq_in.at[other], seq_send.at[other], seq_recv.at[other], (other, b)).wait_recv()
+    seq_sum[...] = jnp.sum(seq_in[...], axis=0)
+
+    def basis_copy(d, block):
+        there = lax.rem(b + d, N_BASIS)
+        block = there if block is None else block
+        return remote(seq_sum, basis_in.at[block], basis_send.at[there], basis_recv.at[block], (s, there))
+
+    for d in range(1, N_BASIS):
+        basis_copy(d, b).start()
+    basis_in[b] = seq_sum[...]
+    for gather in (x_gather, va_gather, vb_gather, wu_gather, wd_gather):
         gather_drain(*gather)
-
+    for d in range(1, N_SEQ):
+        other = lax.rem(s + d, N_SEQ)
+        remote(acc.at[other], seq_in.at[s], seq_send.at[other], seq_recv.at[s], (other, b)).wait_send()
     def drain(k, _):
         for n in range(18):
             h_copy(k, n).wait_send()
         return 0
 
     lax.fori_loop(0, GROUPS, drain, 0)
+    for d in range(1, N_BASIS):
+        basis_copy(d, None).wait_recv()
+    out[...] = jnp.sum(basis_in[...], axis=0)[:6]
+    for d in range(1, N_BASIS):
+        basis_copy(d, b).wait_send()
 
 
 def shards(*blocks):
@@ -482,32 +512,32 @@
             vmem((GROUPS, 2, 64, 1280), BF16),
             vmem((GROUPS, 3, 16, 1280), BF16),
             vmem((GROUPS, 256, 1280), BF16),
-            vmem((16, 2, 320, 320), BF16),
+            vmem((2, 320, 320), BF16),
+            vmem((16, 320, 384), BF16),
+            vmem((16, 320, 256), BF16),
             vmem((2, 128, 5120), BF16),
-            vmem((2, 128, 320), F32),
-            vmem((16, 2, 128, 320), BF16),
+            vmem((2, 320, 128), F32),
+            vmem((16, 320, 128), BF16),
+            vmem((16, 320, 128), BF16),
             vmem((2, 6, 320, 640), BF16),
             vmem((2, 320, 640), F32),
             vmem((2, 6, 320, 640), BF16),
-            vmem((2, 2, 4, 8, 128), F32),
-            vmem((2, 4, 8, 128), F32),
-            vmem((4, 8, 128), F32),
-            vmem((3, 8, 128), F32),
-            vmem((3, 8, 128), F32),
-            vmem((3, 8, 128), F32),
+            vmem((GROUPS, 8, 256), F32),
+            vmem((16, 8, 128), F32),
+            vmem((16, 8, 128), F32),
             vmem((8, 128), F32),
-            vmem((8, 128), F32),
+            vmem((16, 8, 128), F32),
             pltpu.SemaphoreType.DMA((12,)),
             pltpu.SemaphoreType.DMA((4, GROUPS)),
             pltpu.SemaphoreType.DMA((16,)),
-            pltpu.SemaphoreType.DMA((4, GROUPS)),
-            pltpu.SemaphoreType.DMA((16,)),
-            pltpu.SemaphoreType.DMA((4, GROUPS)),
-            pltpu.SemaphoreType.DMA((16,)),
+            pltpu.SemaphoreType.DMA((4, 4, GROUPS)),
+            pltpu.SemaphoreType.DMA((4, 16)),
             pltpu.SemaphoreType.DMA((GROUPS, 18)),
             pltpu.SemaphoreType.DMA((GROUPS, 18)),
-            pltpu.SemaphoreType.DMA((11,)),
-            pltpu.SemaphoreType.DMA((11,)),
+            pltpu.SemaphoreType.DMA((16,)),
+            pltpu.SemaphoreType.DMA((16,)),
+            pltpu.SemaphoreType.DMA((16,)),
+            pltpu.SemaphoreType.DMA((16,)),
         ],
         compiler_params=pltpu.CompilerParams(
             collective_id=0, has_side_effects=True, vmem_limit_bytes=60 * 1024 * 1024

time: 143 us -> 136 us (0.951)
  Pallas kernels: 142 us -> 133 us
    pallas_call x1, Pallas kernels: 142 us -> 133 us  [shards(): pl.pallas_call(kernel, out_shape=jax.ShapeDtypeStruct((6, 128), F32), in_...]
where the time goes in v3:
time: 136 us; the launch traced here: 135 us
  Pallas kernels  133 us (98%)
    pallas_call x1, Pallas kernels, shards(): pl.pallas_call(kernel, out_shape=jax.ShapeDtypeStruct((6, 128), F32), in_...  133 us

profile of v3, /device:TPU:32, one launch (start us, length us, event | category | flops | bytes accessed | tf_op | source)
XLA Modules:
  0.0 134.8 jit_solution(13300491434707824048)
XLA Ops:
  0.0 133.5 %shard_map.118 = f32[6,128]{1,0:T(8,128)} custom-call(bf16[128,5120]{1,0:T(8,128)(2,1)} %up_input.1, bf16[128,640]{1,0:T(8,128)(2,1)} %up_grad.1, bf16[128,640]{1,0:T(8,128)(2,1)} %down_input.1, bf16[128,5120]{1,0:T(8,128)(2,1)} %down_grad.1, bf16[320,320]{1,0:T(8,128)(2,1)} %width_up.1, bf16[320,320]{1,0:T(8,128)(2,1)} %width_down.1, ...), custom_call_target="tpu_custom_call" | custom-call | flops 14000000000 | bytes 12000000 | tf_op jit(solution)/shard_map/pallas_call | solution.py:502
  133.5 1.3 copy.14

commit v4 on v3

--- a/solution.py
+++ b/solution.py
@@ -18,17 +18,17 @@
 O_X, O_PART, O_NEAR, O_OWN, O_SUM, O_SPREAD, O_FORWARD, O_ARRIVE = 0, 0, 1, 2, 3, 4, 5, 6
 VB_START = 3
 VA_MARKS = ((0, 1), (5, 2), (7, 4), (11, 6), (13, 8))
-VB_MARKS = ((0, 1), (9, 2), (11, 4), (15, 6), (17, 8))
+VB_MARKS = ((0, 1), (9, 2), (11, 4), (13, 6), (15, 8))
 VAC_MARKS = ((0, 0), (7, 2), (9, 4), (13, 6), (15, 8))
-VBC_MARKS = ((0, 0), (13, 2), (15, 4), (17, 6), (19, 8))
+VBC_MARKS = ((0, 0), (13, 2), (15, 6), (17, 8))
 WU_START = 15
-WU_MARKS = ((0, 1), (17, 2), (18, 6), (19, 8))
-WUC_MARKS = ((0, 0), (19, 8))
-WD_START = 19
-WD_MARKS = ((0, 1), (20, 2), (21, 6), (22, 8))
-WDC_MARKS = ((0, 0), (22, 8))
-SU_START = 19
-SD_START = 22
+WU_MARKS = ((0, 1), (16, 2), (17, 6), (18, 8))
+WUC_MARKS = ((0, 0), (18, 8))
+WD_START = 17
+WD_MARKS = ((0, 1), (18, 2), (19, 6), (20, 8))
+WDC_MARKS = ((0, 0), (20, 8))
+SU_START = 18
+SD_START = 20
 RATE = 2
 
 

time: 136 us -> 135 us (level)
  no operation moved by 1% of the time
where the time goes in v4:
time: 135 us; the launch traced here: 133 us
  Pallas kernels  132 us (98%)
    pallas_call x1, Pallas kernels, shards(): pl.pallas_call(kernel, out_shape=jax.ShapeDtypeStruct((6, 128), F32), in_...  132 us

profile of v4, /device:TPU:32, one launch (start us, length us, event | category | flops | bytes accessed | tf_op | source)
XLA Modules:
  0.0 133.4 jit_solution(3356063185094598928)
XLA Ops:
  0.0 132.1 %shard_map.118 = f32[6,128]{1,0:T(8,128)} custom-call(bf16[128,5120]{1,0:T(8,128)(2,1)} %up_input.1, bf16[128,640]{1,0:T(8,128)(2,1)} %up_grad.1, bf16[128,640]{1,0:T(8,128)(2,1)} %down_input.1, bf16[128,5120]{1,0:T(8,128)(2,1)} %down_grad.1, bf16[320,320]{1,0:T(8,128)(2,1)} %width_up.1, bf16[320,320]{1,0:T(8,128)(2,1)} %width_down.1, ...), custom_call_target="tpu_custom_call" | custom-call | flops 14000000000 | bytes 12000000 | tf_op jit(solution)/shard_map/pallas_call | solution.py:502
  132.1 1.3 copy.14
